TPU v7x, 32 devices: a whole 2x2x4 slice. The times are simulated.
32 devices in a mesh: group: 2 (over x), block: 16 (over z, y, core).
Axes of the slice: x: 2, y: 2, z: 4, core: 2. Of those that a mesh axis runs over, the one named last changes fastest.
Arguments:
- block_factor: bfloat16 [4096, 256], P(('group', 'block')), parts along dimension 0, may hold values from 0.0049743652 to 0.049804688
- hour_factor: bfloat16 [16384, 256], P(('group', 'block')), parts along dimension 0, may hold values from 0.0049743652 to 0.049804688
- port_factor: bfloat16 [131072, 256], P(('group', 'block')), parts along dimension 0, may hold values from 0.0049743652 to 0.049804688
- tile_count: int32 [32], P(('group', 'block')), parts along dimension 0, may hold values from 32 to 64, as said below
- hour_tiles: int32 [2048], P(('group', 'block')), parts along dimension 0, may hold values from 0 to 63, as said below
- port_tiles: int32 [2048], P(('group', 'block')), parts along dimension 0, may hold values from 0 to 511, as said below
- entry_coords: int32 [2048, 3, 256], P(('group', 'block')), parts along dimension 0, may hold values from 0 to 127
- entry_counts: int32 [2048, 256], P(('group', 'block')), parts along dimension 0, may hold values from 1 to 8
Outputs:
- block_grad: float32 [4096, 256], P(('group', 'block')), parts along dimension 0
- hour_grad: float32 [16384, 256], P(('group', 'block')), parts along dimension 0
- port_grad: float32 [131072, 256], P(('group', 'block')), parts along dimension 0
There are 2 independent parts, one for each index of `group`. A program takes and returns all parts, laid end to end along the dimension named above; each array names one. Nothing has to cross between parts.
Inputs may be any that keep to these rules, and one draw needn't show every extreme that they name: Each device uses slots 0 to tile_count - 1 of its 64; some device uses all 64. `hour_tiles`: among the 64 slots of one device, live or not, at most 4 name hour tiles whose rows one device holds (device o holds hour tiles o * 4 to o * 4 + 3), and some device reaches 4. `port_tiles`: among the 64 slots of one device, live or not, at most 4 name port tiles whose rows one device holds (device o holds port tiles o * 32 to o * 32 + 31), and some device reaches 4. `entry_coords`: entries of one tile may name the same cell more than once; each is a term of its own.
All inputs are finite; a program needn't handle non-finite values.
Results may differ from a plain program's by a relative error of at most 0.00049.
Values may be sent and summed in bfloat16 or wider, within the bound.
A program may use at most 128 MiB of HBM per device.

v0:
```python
import jax
import jax.numpy as jnp
from jax import lax
from jax.sharding import PartitionSpec as P


def tile_terms(own_rows, hour_block, port_block, offsets, counts, group_live):
    tile_side = own_rows.shape[1]
    cells = jnp.arange(tile_side, dtype=jnp.int32)
    pick_a = (offsets[:, 0, :, None] == cells).astype(jnp.bfloat16)
    pick_b = (offsets[:, 1, :, None] == cells).astype(jnp.bfloat16)
    pick_c = (offsets[:, 2, :, None] == cells).astype(jnp.bfloat16)
    rows_a = jnp.einsum("gep,gpr->ger", pick_a, own_rows, preferred_element_type=jnp.float32)
    rows_b = jnp.einsum("gep,gpr->ger", pick_b, hour_block, preferred_element_type=jnp.float32)
    rows_c = jnp.einsum("gep,gpr->ger", pick_c, port_block, preferred_element_type=jnp.float32)
    model = jnp.sum(rows_a * rows_b * rows_c, axis=-1)
    model = jnp.where(group_live[:, None], model, 1.0)
    ratio = jnp.where(group_live[:, None], counts.astype(jnp.float32) / model, 0.0)
    term_a = (ratio[..., None] * rows_b * rows_c).astype(jnp.bfloat16)
    term_b = (ratio[..., None] * rows_a * rows_c).astype(jnp.bfloat16)
    term_c = (ratio[..., None] * rows_a * rows_b).astype(jnp.bfloat16)
    back_a = jnp.einsum("gep,ger->gpr", pick_a, term_a, preferred_element_type=jnp.float32)
    back_b = jnp.einsum("gep,ger->gpr", pick_b, term_b, preferred_element_type=jnp.float32)
    back_c = jnp.einsum("gep,ger->gpr", pick_c, term_c, preferred_element_type=jnp.float32)
    sum_a = jnp.sum(own_rows.astype(jnp.float32), axis=1)
    sum_b = jnp.sum(hour_block.astype(jnp.float32), axis=1)
    sum_c = jnp.sum(port_block.astype(jnp.float32), axis=1)
    weight = group_live.astype(jnp.float32)[:, None, None]
    part_a = weight * (sum_b * sum_c)[:, None, :] - back_a
    part_b = weight * (sum_a * sum_c)[:, None, :] - back_b
    part_c = weight * (sum_a * sum_b)[:, None, :] - back_c
    return (part_a, part_b, part_c)


def tile_loop(block_factor, hour_rows, port_rows, entry_coords, entry_counts, live_slot):
    slot_count, tile_side, rank_width = hour_rows.shape
    group = min(8, slot_count)

    def visit(step, carry):
        block_acc, hour_part, port_part = carry
        begin = step * group
        group_live = lax.dynamic_slice_in_dim(live_slot, begin, group)

        def compute(offset_start):
            hour_block = lax.dynamic_slice_in_dim(hour_rows, offset_start, group)
            port_block = lax.dynamic_slice_in_dim(port_rows, offset_start, group)
            offsets = lax.dynamic_slice_in_dim(entry_coords, offset_start, group)
            counts = lax.dynamic_slice_in_dim(entry_counts, offset_start, group)
            own_rows = jnp.broadcast_to(block_factor, (group, tile_side, rank_width))
            part_a, part_b, part_c = tile_terms(
                own_rows, hour_block, port_block, offsets, counts, group_live
            )
            return (jnp.sum(part_a, axis=0), part_b, part_c)

        def nothing(offset_start):
            empty = jnp.zeros((group, tile_side, rank_width), jnp.float32)
            return (jnp.zeros((tile_side, rank_width), jnp.float32), empty, empty)

        sum_a, part_b, part_c = lax.cond(jnp.any(group_live), compute, nothing, begin)
        block_acc = block_acc + sum_a
        hour_part = lax.dynamic_update_slice_in_dim(hour_part, part_b, begin, 0)
        port_part = lax.dynamic_update_slice_in_dim(port_part, part_c, begin, 0)
        return (block_acc, hour_part, port_part)

    empty_slots = jnp.zeros((slot_count, tile_side, rank_width), jnp.float32)
    start = (jnp.zeros((tile_side, rank_width), jnp.float32), empty_slots, empty_slots)
    return lax.fori_loop(0, slot_count // group, visit, start)


def slot_positions(owner, live_slot, per_peer, slot_total):
    count = owner.shape[0]
    order = jnp.arange(count, dtype=jnp.int32)
    earlier = (
        (order[None, :] < order[:, None]) & (owner[None, :] == owner[:, None]) & live_slot[None, :]
    )
    before = jnp.sum(earlier.astype(jnp.int32), axis=1)
    return jnp.where(live_slot, owner * per_peer + before, slot_total)


def ask_buffer(positions, local_index, slot_total):
    hits = positions[:, None] == jnp.arange(slot_total, dtype=jnp.int32)[None, :]
    return jnp.sum(jnp.where(hits, (local_index + 1)[:, None], 0), axis=0)


def serve_rows(asked, factor, tile_side):
    rank_width = factor.shape[1]
    wanted = asked.reshape(-1)
    stacked = factor.reshape(-1, tile_side, rank_width)
    picked = jnp.take(stacked, jnp.maximum(wanted - 1, 0), axis=0)
    picked = jnp.where((wanted > 0)[:, None, None], picked, jnp.zeros_like(picked))
    return picked.reshape(asked.shape[0], asked.shape[1], tile_side, rank_width)


def pick_rows(arrived, positions, tile_side):
    flat = arrived.reshape(-1, tile_side, arrived.shape[-1])
    return jnp.take(flat, jnp.clip(positions, 0, flat.shape[0] - 1), axis=0)


def send_buffer(partial_value, positions, devices, per_peer):
    holder = jnp.zeros((devices * per_peer,) + partial_value.shape[1:], jnp.float32)
    holder = holder.at[positions].add(partial_value, mode="drop")
    return holder.reshape((devices, per_peer) + partial_value.shape[1:])


def collect(returned, asked, local_count):
    tile_side = returned.shape[2]
    rank_width = returned.shape[3]
    wanted = asked.reshape(-1)
    chooser = (wanted[:, None] == jnp.arange(1, local_count + 1, dtype=jnp.int32)[None, :]).astype(
        jnp.float32
    )
    total = jnp.einsum(
        "qt,qpr->tpr",
        chooser,
        returned.reshape(-1, tile_side, rank_width),
        precision=lax.Precision.HIGHEST,
    )
    return total.reshape(local_count * tile_side, rank_width)


def local(
    block_factor,
    hour_factor,
    port_factor,
    tile_count,
    hour_tiles,
    port_tiles,
    entry_coords,
    entry_counts,
):
    devices = lax.axis_size("block")
    tile_side = block_factor.shape[0]
    rank_width = block_factor.shape[1]
    slot_count = hour_tiles.shape[0]
    port_local = port_factor.shape[0] // tile_side
    per_peer = (slot_count + devices - 1) // devices
    slot_total = devices * per_peer
    live_slot = jnp.arange(slot_count, dtype=jnp.int32) < tile_count[0]
    port_pos = slot_positions(port_tiles // port_local, live_slot, per_peer, slot_total)
    port_ask = ask_buffer(port_pos, port_tiles % port_local, slot_total).reshape(devices, per_peer)
    port_asked = lax.all_to_all(port_ask, "block", split_axis=0, concat_axis=0, tiled=True)
    port_sent = lax.all_to_all(
        serve_rows(port_asked, port_factor, tile_side),
        "block",
        split_axis=0,
        concat_axis=0,
        tiled=True,
    )
    whole_hours = lax.all_gather(hour_factor, "block", axis=0, tiled=True)
    hour_rows = jnp.take(whole_hours.reshape(-1, tile_side, rank_width), hour_tiles, axis=0)
    port_rows = pick_rows(port_sent, port_pos, tile_side)
    block_acc, hour_part, port_part = tile_loop(
        block_factor, hour_rows, port_rows, entry_coords, entry_counts, live_slot
    )
    port_back = lax.all_to_all(
        send_buffer(port_part, port_pos, devices, per_peer),
        "block",
        split_axis=0,
        concat_axis=0,
        tiled=True,
    )
    hour_total = whole_hours.shape[0] // tile_side
    chooser = (hour_tiles[:, None] == jnp.arange(hour_total, dtype=jnp.int32)[None, :]).astype(
        jnp.float32
    )
    dense_hours = jnp.einsum("st,spr->tpr", chooser, hour_part, precision=lax.Precision.HIGHEST)
    hour_grad = lax.psum_scatter(
        dense_hours.reshape(-1, rank_width), "block", scatter_dimension=0, tiled=True
    )
    port_grad = collect(port_back, port_asked, port_local)
    factor_scale = 1.0 / tile_side
    return (block_acc * factor_scale, hour_grad * factor_scale, port_grad * factor_scale)


def solution(mesh):
    in_specs = (
        P(("group", "block"), None),
        P(("group", "block"), None),
        P(("group", "block"), None),
        P(("group", "block")),
        P(("group", "block")),
        P(("group", "block")),
        P(("group", "block"), None, None),
        P(("group", "block"), None),
    )
    out_specs = (
        P(("group", "block"), None),
        P(("group", "block"), None),
        P(("group", "block"), None),
    )
    return jax.shard_map(local, mesh=mesh, in_specs=in_specs, out_specs=out_specs, check_vma=False)
```

profile of v0, /device:TPU:19, one launch (start us, length us, event | category | flops | bytes accessed | tf_op | source)
XLA Modules:
  0.0 582.2 jit_solution(757965580083013455)
XLA Ops:
  9.6 6.5 %all-to-all-start = ((s32[16,1,4]{2,1,0:T(1,128)}), s32[16,1,4]{2,1,0:T(1,128)S(1)}, u32[]{:S(2)}, u32[]{:S(2)}) async-start(s32[16,1,4]{2,1,0:T(1,128)} %bitcast.5), calls=%async_computation | async-start | bytes 16384 | tf_op jit(solution)/shard_map/all_to_all | solution.py:141
  16.9 3.0 all-to-all-done
  20.4 2.8 gather_fusion
  23.2 3.9 select_select_fusion
  27.1 7.2 %all-to-all-start.1 = ((bf16[16,4,128,256]{3,2,1,0:T(8,128)(2,1)}), bf16[16,4,128,256]{3,2,1,0:T(8,128)(2,1)}, u32[]{:S(2)}, u32[]{:S(2)}) async-start(bf16[16,4,128,256]{3,2,1,0:T(8,128)(2,1)} %select_select_fusion), calls=%async_computation.1 | async-start | bytes 8388608 | tf_op jit(solution)/shard_map/all_to_all | solution.py:142
  34.5 82.3 %all-gather.2.cloned.1.call-done = bf16[8192,256]{1,0:T(8,128)(2,1)} async-done(((bf16[512,256]{1,0:T(8,128)(2,1)}), bf16[8192,256]{1,0:T(8,128)(2,1)}) %all-gather.2.cloned.1.call-update) | async-done | bytes 4194320 | tf_op jit(solution)/shard_map/all_gather | solution.py:149
  116.9 5.0 gather_fusion.1
  121.9 4.6 broadcast_select_fusion.1
  126.5 6.3 %copy.109 = bf16[64,128,256]{1,2,0:T(8,128)(2,1)} copy(bf16[64,128,256]{2,1,0:T(8,128)(2,1)} %broadcast_select_fusion.1) | data formatting | bytes 8388608
  132.9 14.2 %all-to-all-done.1 = bf16[16,4,128,256]{3,2,1,0:T(8,128)(2,1)} async-done(((bf16[16,4,128,256]{3,2,1,0:T(8,128)(2,1)}), bf16[16,4,128,256]{3,2,1,0:T(8,128)(2,1)}, u32[]{:S(2)}, u32[]{:S(2)}) %all-to-all-start.1) | async-done | bytes 4194336 | tf_op jit(solution)/shard_map/all_to_all | solution.py:142
  147.0 5.0 gather_fusion.2
  152.1 4.6 broadcast_select_fusion
  156.7 6.4 %copy.110 = bf16[64,128,256]{1,2,0:T(8,128)(2,1)} copy(bf16[64,128,256]{2,1,0:T(8,128)(2,1)} %broadcast_select_fusion) | data formatting | bytes 8388608
  163.1 4.2 broadcast.141.clone.1
  167.3 4.3 broadcast.141.clone
  171.6 75.9 %while.18 = (s32[]{:T(128)}, f32[128,256]{1,0:T(8,128)S(1)}, f32[64,128,256]{2,0,1:T(8,128)}, f32[64,128,256]{2,1,0:T(8,128)}, pred[64]{0:T(512)(128)(4,1)S(1)},...) while((s32[]{:T(128)}, f32[128,256]{1,0:T(8,128)S(1)}, ...), condition=%wide.region_11.13_spmd.clone, body=%wide.region_2.12_spmd.clone.sunk | while | flops 815380224 | bytes 32352732 | solution.py:67
  173.0 8.4 %conditional.3 = (f32[128,256]{1,0:T(8,128)S(1)}, f32[8,128,256]{2,1,0:T(8,128)S(1)}, f32[8,128,256]{2,1,0:T(8,128)S(1)}) conditional(s32[]{:T(128)} %convert_element_type.54, () %tuple.68, (pred[8]{0:T(512)(128)(4,1)S(1)}, s32[]{:T(128)}, bf16[64,128,256]{1,2,0:T(8,128)(2,1)}, bf16[64,128,256]{1,2,0:T(8,128)(2,1)}, s32[64,3,256]{2,0,1:T(8,128)}, ...), branch_computations={%region_4.5_spmd, %region_5.11_spmd} | conditional | flops 815314688 | bytes 27764926 | solution.py:59
  173.1 1.6 convert_reduce_fusion
  177.5 1.6 multiply_reduce_fusion
  181.4 1.7 copy_dynamic-update-slice_fusion.2
  185.5 8.4 %conditional.3 = (f32[128,256]{1,0:T(8,128)S(1)}, f32[8,128,256]{2,1,0:T(8,128)S(1)}, f32[8,128,256]{2,1,0:T(8,128)S(1)}) conditional(s32[]{:T(128)} %convert_element_type.54, () %tuple.68, (pred[8]{0:T(512)(128)(4,1)S(1)}, s32[]{:T(128)}, bf16[64,128,256]{1,2,0:T(8,128)(2,1)}, bf16[64,128,256]{1,2,0:T(8,128)(2,1)}, s32[64,3,256]{2,0,1:T(8,128)}, ...), branch_computations={%region_4.5_spmd, %region_5.11_spmd} | conditional | flops 815314688 | bytes 27764926 | solution.py:59
  190.0 1.6 multiply_reduce_fusion
  194.0 1.7 copy_dynamic-update-slice_fusion.2
  198.1 8.4 %conditional.3 = (f32[128,256]{1,0:T(8,128)S(1)}, f32[8,128,256]{2,1,0:T(8,128)S(1)}, f32[8,128,256]{2,1,0:T(8,128)S(1)}) conditional(s32[]{:T(128)} %convert_element_type.54, () %tuple.68, (pred[8]{0:T(512)(128)(4,1)S(1)}, s32[]{:T(128)}, bf16[64,128,256]{1,2,0:T(8,128)(2,1)}, bf16[64,128,256]{1,2,0:T(8,128)(2,1)}, s32[64,3,256]{2,0,1:T(8,128)}, ...), branch_computations={%region_4.5_spmd, %region_5.11_spmd} | conditional | flops 815314688 | bytes 27764926 | solution.py:59
  202.6 1.6 multiply_reduce_fusion
  206.6 1.7 copy_dynamic-update-slice_fusion.2
  210.7 8.4 %conditional.3 = (f32[128,256]{1,0:T(8,128)S(1)}, f32[8,128,256]{2,1,0:T(8,128)S(1)}, f32[8,128,256]{2,1,0:T(8,128)S(1)}) conditional(s32[]{:T(128)} %convert_element_type.54, () %tuple.68, (pred[8]{0:T(512)(128)(4,1)S(1)}, s32[]{:T(128)}, bf16[64,128,256]{1,2,0:T(8,128)(2,1)}, bf16[64,128,256]{1,2,0:T(8,128)(2,1)}, s32[64,3,256]{2,0,1:T(8,128)}, ...), branch_computations={%region_4.5_spmd, %region_5.11_spmd} | conditional | flops 815314688 | bytes 27764926 | solution.py:59
  215.2 1.6 multiply_reduce_fusion
  219.2 1.7 copy_dynamic-update-slice_fusion.2
  223.3 8.4 %conditional.3 = (f32[128,256]{1,0:T(8,128)S(1)}, f32[8,128,256]{2,1,0:T(8,128)S(1)}, f32[8,128,256]{2,1,0:T(8,128)S(1)}) conditional(s32[]{:T(128)} %convert_element_type.54, () %tuple.68, (pred[8]{0:T(512)(128)(4,1)S(1)}, s32[]{:T(128)}, bf16[64,128,256]{1,2,0:T(8,128)(2,1)}, bf16[64,128,256]{1,2,0:T(8,128)(2,1)}, s32[64,3,256]{2,0,1:T(8,128)}, ...), branch_computations={%region_4.5_spmd, %region_5.11_spmd} | conditional | flops 815314688 | bytes 27764926 | solution.py:59
  227.8 1.6 multiply_reduce_fusion
  231.7 1.6 copy_dynamic-update-slice_fusion.2
  236.0 1.7 copy_dynamic-update-slice_fusion.2
  240.4 1.6 copy_dynamic-update-slice_fusion.2
  244.8 1.7 copy_dynamic-update-slice_fusion.2
  247.5 4.2 broadcast.141
  251.7 19.0 %scatter_fusion = f32[64,128,256]{2,1,0:T(8,128)} fusion(f32[64,128,256]{2,1,0:T(8,128)} %broadcast.141, s32[64]{0:T(128)S(1)} %get-tuple-element.320, f32[64,128,256]{2,1,0:T(8,128)} %get-tuple-element.201), kind=kCustom, calls=%fused_computation.3 | custom fusion | flops 2097152 | bytes 25166080 | tf_op jit(solution)/shard_map/scatter-add | solution.py:101
  270.8 12.2 %copy.114 = f32[16,4,128,256]{3,1,2,0:T(4,128)} copy(f32[16,4,128,256]{3,2,1,0:T(8,128)} %bitcast.34) | data formatting | bytes 16777216 | tf_op jit(solution)/shard_map/reshape | solution.py:102
  282.9 29.5 %all-to-all-start.2 = ((f32[16,4,128,256]{3,1,2,0:T(4,128)}), f32[16,4,128,256]{3,1,2,0:T(4,128)}, u32[]{:S(2)}, u32[]{:S(2)}) async-start(f32[16,4,128,256]{3,1,2,0:T(4,128)} %copy.114), calls=%async_computation.3 | async-start | bytes 16777216 | tf_op jit(solution)/shard_map/all_to_all | solution.py:155
  312.5 7.1 %fusion.21 = f32[64,128,256]{2,0,1:T(8,128)S(1)} fusion(f32[64,128,256]{2,0,1:T(8,128)} %get-tuple-element.200, s32[64]{0:T(128)S(1)} %copy-done.3), kind=kOutput, calls=%fused_computation.59 | convolution fusion | flops 1610616832 | bytes 16777472 | tf_op jit(solution)/shard_map/st,spr->tpr/dot_general | solution.py:166
  319.6 8.1 %copy.113 = f32[64,128,256]{2,1,0:T(8,128)} copy(f32[64,128,256]{2,0,1:T(8,128)S(1)} %fusion.21) | data formatting | bytes 16777216 | tf_op jit(solution)/shard_map/st,spr->tpr/dot_general | solution.py:166
  329.7 200.4 %reduce-scatter.2.cloned.1.call-done = f32[512,256]{1,0:T(8,128)} async-done(((f32[8192,256]{1,0:T(8,128)}), f32[512,256]{1,0:T(8,128)}) %reduce-scatter.2.cloned.1.call-update) | async-done | bytes 524304 | tf_op jit(solution)/shard_map/reduce_scatter | solution.py:167
  530.2 1.9 broadcast_multiply_fusion
  532.0 13.7 %all-to-all-done.2 = f32[16,4,128,256]{3,1,2,0:T(4,128)} async-done(((f32[16,4,128,256]{3,1,2,0:T(4,128)}), f32[16,4,128,256]{3,1,2,0:T(4,128)}, u32[]{:S(2)}, u32[]{:S(2)}) %all-to-all-start.2) | async-done | bytes 8388640 | tf_op jit(solution)/shard_map/all_to_all | solution.py:155
  545.7 9.1 %copy.115 = f32[16,4,128,256]{3,1,0,2:T(4,128)} copy(f32[16,4,128,256]{3,1,2,0:T(4,128)} %all-to-all-done.2) | data formatting | bytes 16777216 | tf_op jit(solution)/shard_map/all_to_all | solution.py:155
  554.8 10.0 %reshape.176 = f32[64,128,256]{2,0,1:T(8,128)} reshape(f32[16,4,128,256]{3,1,0,2:T(4,128)} %copy.115) | data formatting | bytes 16777216 | tf_op jit(solution)/shard_map/reshape | solution.py:115
  564.8 6.1 %convolution_multiply_fusion = f32[32,128,256]{2,0,1:T(8,128)S(1)} fusion(f32[64,128,256]{2,0,1:T(8,128)} %reshape.176, s32[64]{0:T(128)S(1)} %reshape.174, s32[32]{0:T(128)S(1)} %iota_add_fusion), kind=kOutput, calls=%fused_computation.48 | convolution fusion | flops 806356992 | bytes 12583296 | tf_op jit(solution)/shard_map/qt,qpr->tpr/dot_general | solution.py:112
  570.9 4.4 copy.116
  (128 shorter events, 52.8 us)
Async XLA Ops:
  7.2 13.2 %copy-start = (bf16[4096,256]{1,0:T(8,128)(2,1)S(1)}, bf16[4096,256]{1,0:T(8,128)(2,1)}, u32[]{:S(2)}) copy-start(bf16[4096,256]{1,0:T(8,128)(2,1)} %param.16) | copy-start | bytes 6291460
  9.6 10.2 %all-to-all-start = ((s32[16,1,4]{2,1,0:T(1,128)}), s32[16,1,4]{2,1,0:T(1,128)S(1)}, u32[]{:S(2)}, u32[]{:S(2)}) async-start(s32[16,1,4]{2,1,0:T(1,128)} %bitcast.5), calls=%async_computation | async-start | bytes 16384 | tf_op jit(solution)/shard_map/all_to_all | solution.py:141
  16.1 100.7 %all-gather.2.cloned.1.call-start = ((), (), s32[]{:S(2)}) async-start(), calls=%async_computation.4 | async-start | bytes 4456448 | tf_op jit(solution)/shard_map/all_gather | solution.py:149
  27.1 7.2 %copy-start.2 = (bf16[128,256]{1,0:T(8,128)(2,1)S(1)}, bf16[128,256]{1,0:T(8,128)(2,1)}, u32[]{:S(2)}) copy-start(bf16[128,256]{1,0:T(8,128)(2,1)} %param.14) | copy-start | bytes 196612
  27.1 7.3 %copy-start.3 = (s32[64]{0:T(128)S(1)}, s32[64]{0:T(128)}, u32[]{:S(2)}) copy-start(s32[64]{0:T(128)} %param.18) | copy-start | bytes 772
  27.1 119.9 %all-to-all-start.1 = ((bf16[16,4,128,256]{3,2,1,0:T(8,128)(2,1)}), bf16[16,4,128,256]{3,2,1,0:T(8,128)(2,1)}, u32[]{:S(2)}, u32[]{:S(2)}) async-start(bf16[16,4,128,256]{3,2,1,0:T(8,128)(2,1)} %select_select_fusion), calls=%async_computation.1 | async-start | bytes 8388608 | tf_op jit(solution)/shard_map/all_to_all | solution.py:142
  282.9 262.8 %all-to-all-start.2 = ((f32[16,4,128,256]{3,1,2,0:T(4,128)}), f32[16,4,128,256]{3,1,2,0:T(4,128)}, u32[]{:S(2)}, u32[]{:S(2)}) async-start(f32[16,4,128,256]{3,1,2,0:T(4,128)} %copy.114), calls=%async_computation.3 | async-start | bytes 16777216 | tf_op jit(solution)/shard_map/all_to_all | solution.py:155
  312.5 217.7 %reduce-scatter.2.cloned.1.call-start = ((), (), s32[]{:S(2)}) async-start(), calls=%async_computation.5 | async-start | bytes 8912896 | tf_op jit(solution)/shard_map/reduce_scatter | solution.py:167
  564.8 10.6 %copy-start.1 = (bf16[4096,256]{1,0:T(8,128)(2,1)S(1)}, bf16[4096,256]{1,0:T(8,128)(2,1)}, u32[]{:S(2)}) copy-start(bf16[4096,256]{1,0:T(8,128)(2,1)} %param.16) | copy-start | bytes 6291460
Sparse Core Ops, SparseCore 0:
  19.1 97.6 all-gather.1
  327.9 202.2 reduce-scatter.1
where the time goes:
time: 585 us; the launch traced here: 582 us
  waiting for transfers between devices  314 us (54%)
  local copies, waits for them, and re-layouts  110 us (19%)
  other arithmetic  55 us (9%)
  starting transfers between devices  43.3 us (7%)
  matrix products  38.7 us (7%)
  between operations  15 us (3%)
  loops' own time  5.88 us (1%)
    reduce_scatter x1, waiting for transfers between devices, local(): lax.psum_scatter(dense_hours.reshape(-1, rank_width), 'block', scatter_di...  200 us
    all_gather x1, waiting for transfers between devices, local(): whole_hours = lax.all_gather(hour_factor, 'block', axis=0, tiled=True)  82.3 us
    all_to_all x1, starting transfers between devices, local(): lax.all_to_all(send_buffer(port_part, port_pos, devices, per_peer), 'bloc...  29.5 us
    scatter-add x1, other arithmetic, send_buffer(): holder = holder.at[positions].add(partial_value, mode='drop')  19 us
    all_to_all x1, waiting for transfers between devices, local(): lax.all_to_all(serve_rows(port_asked, port_factor, tile_side), 'block', s...  14.2 us
    all_to_all x1, waiting for transfers between devices, local(): lax.all_to_all(send_buffer(port_part, port_pos, devices, per_peer), 'bloc...  13.7 us
    dynamic_update_slice x8, local copies, waits for them, and re-layouts, visit(): hour_part = lax.dynamic_update_slice_in_dim(hour_part, part_b, begin, 0)  13.4 us
    another operation x12, local copies, waits for them, and re-layouts  13.3 us
  transfers between devices with their start and end apart: 5, of which 5 were waited for; matrix products, arithmetic and copies ran while one was open for 7% of the time, Pallas kernels for 0%

commit v1 on v0

v1 whole, which is shorter than its diff:
```python
import functools

import jax
import jax.numpy as jnp
from jax import lax
from jax.experimental import pallas as pl
from jax.experimental.pallas import tpu as pltpu
from jax.sharding import PartitionSpec as P

MESH = pl.DeviceIdType.MESH
PIECES = 2


def ring(devices):
    chips = devices // 2
    half = chips // 2
    me = lax.axis_index("block")
    group = lax.axis_index("group")
    chip = me // 2
    core = me % 2
    odd = chip % 2
    place = (1 - odd) * (chip // 2) + odd * (chips - (chip + 1) // 2)

    def member(offset, lane):
        spot = (place + offset + chips) % chips
        back = spot // half
        at = (1 - back) * (2 * spot) + back * (2 * (chips - spot) - 1)
        return at * 2 + lane

    return group, me, core, member


def greet(group, partners):
    barrier = pltpu.get_barrier_semaphore()
    for partner in partners:
        pl.semaphore_signal(barrier, inc=1, device_id=(group, partner), device_id_type=MESH)
    pl.semaphore_wait(barrier, len(partners))


def gather_kernel(devices, *refs):
    count = (len(refs) - 7) // 2
    ins, outs = refs[:count], refs[count : 2 * count]
    local_sem, send_sem, recv_sem, pair_send, pair_recv, own_send, own_recv = refs[2 * count :]
    reach = devices // 4
    group, me, core, member = ring(devices)
    sibling = member(0, 1 - core)
    greet(group, (member(-1, core), member(1, core), sibling))

    started = []
    for a in range(count):
        keep = pltpu.make_async_copy(ins[a], outs[a].at[me], local_sem.at[a])
        keep.start()
        started.append(keep)

    def hop(a, way, step, piece):
        rows = ins[a].shape[0] // PIECES
        sign = 1 - 2 * way
        origin = member(-sign * (step - 1), core)
        part = pl.ds(piece * rows, rows)
        here = ins[a].at[part] if step == 1 else outs[a].at[origin, part]
        return pltpu.make_async_remote_copy(
            src_ref=here,
            dst_ref=outs[a].at[origin, part],
            send_sem=send_sem.at[a, way, step - 1, piece],
            recv_sem=recv_sem.at[a, way, step - 1, piece],
            device_id=(group, member(sign, core)),
            device_id_type=MESH,
        )

    def share(a, way, step, piece, lane):
        rows = ins[a].shape[0] // PIECES
        sign = 1 - 2 * way
        origin = member(-sign * step, lane)
        part = pl.ds(piece * rows, rows)
        return pltpu.make_async_remote_copy(
            src_ref=outs[a].at[origin, part],
            dst_ref=outs[a].at[origin, part],
            send_sem=pair_send.at[a, way, step - 1, piece],
            recv_sem=pair_recv.at[a, way, step - 1, piece],
            device_id=(group, sibling),
            device_id_type=MESH,
        )

    def own_share(a):
        return pltpu.make_async_remote_copy(
            src_ref=ins[a],
            dst_ref=outs[a].at[me],
            send_sem=own_send.at[a],
            recv_sem=own_recv.at[a],
            device_id=(group, sibling),
            device_id_type=MESH,
        )

    def plan(step):
        pairs = []
        for turn in range(PIECES):
            for way in range(2):
                piece = turn if way == 0 else 1 - turn
                if step < reach or turn == 0:
                    pairs.append((way, piece))
        return pairs

    sends = []
    for way, piece in plan(1):
        for a in range(count):
            copy = hop(a, way, 1, piece)
            copy.start()
            sends.append(copy)
    for a in range(count):
        copy = own_share(a)
        copy.start()
        sends.append(copy)
    for step in range(1, reach + 1):
        onward = plan(step + 1) if step < reach else []
        for way, piece in plan(step):
            for a in range(count):
                hop(a, way, step, piece).wait_recv()
                if (way, piece) in onward:
                    copy = hop(a, way, step + 1, piece)
                    copy.start()
                    sends.append(copy)
                copy = share(a, way, step, piece, core)
                copy.start()
                sends.append(copy)
    for a in range(count):
        own_share(a).wait_recv()
    for step in range(1, reach + 1):
        for way, piece in plan(step):
            for a in range(count):
                share(a, way, step, piece, 1 - core).wait_recv()
    for copy in sends:
        copy.wait_send()
    for copy in started:
        copy.wait()


def gather(devices, *arrays):
    reach = devices // 4
    count = len(arrays)
    sems = (count, 2, reach, PIECES)
    return pl.pallas_call(
        functools.partial(gather_kernel, devices),
        out_shape=[jax.ShapeDtypeStruct((devices,) + x.shape, x.dtype) for x in arrays],
        in_specs=[pl.BlockSpec(memory_space=pl.ANY)] * count,
        out_specs=[pl.BlockSpec(memory_space=pl.ANY)] * count,
        scratch_shapes=[
            pltpu.SemaphoreType.DMA((count,)),
            pltpu.SemaphoreType.DMA(sems),
            pltpu.SemaphoreType.DMA(sems),
            pltpu.SemaphoreType.DMA(sems),
            pltpu.SemaphoreType.DMA(sems),
            pltpu.SemaphoreType.DMA((count,)),
            pltpu.SemaphoreType.DMA((count,)),
        ],
        compiler_params=pltpu.CompilerParams(collective_id=0, has_side_effects=True),
        name="gather_rows",
    )(*arrays)


def scatter_kernel(devices, scale, part, hour_out, block_out, mate, held, *sems):
    send_sem, recv_sem, pair_send, pair_recv = sems
    reach = devices // 4
    chips = devices // 2
    rows = part.shape[1] // PIECES
    group, me, core, member = ring(devices)
    sibling = member(0, 1 - core)
    greet(group, (member(-1, core), member(1, core), sibling))

    def swap(offset):
        return pltpu.make_async_remote_copy(
            src_ref=part.at[member(offset, 1 - core)],
            dst_ref=mate.at[offset % chips],
            send_sem=pair_send.at[offset % chips],
            recv_sem=pair_recv.at[offset % chips],
            device_id=(group, sibling),
            device_id_type=MESH,
        )

    def hop(way, step, piece):
        sign = 1 - 2 * way
        area = pl.ds(piece * rows, rows)
        here = mate.at[reach, area] if step == 1 else held.at[way, step - 2, area]
        return pltpu.make_async_remote_copy(
            src_ref=here,
            dst_ref=held.at[way, step - 1, area],
            send_sem=send_sem.at[way, step - 1, piece],
            recv_sem=recv_sem.at[way, step - 1, piece],
            device_id=(group, member(sign, core)),
            device_id_type=MESH,
        )

    order = [reach]
    for step in range(2, reach + 1):
        order += [reach - step + 1, -(reach - step + 1)]
    order.append(0)
    swaps = [swap(offset) for offset in order]
    for copy in swaps:
        copy.start()
    arrived = {offset: copy for offset, copy in zip(order, swaps)}

    sends = []
    arrived[reach].wait_recv()
    far = member(reach, core)
    for way in range(2):
        area = pl.ds(way * rows, rows)
        mate[reach, area] = mate[reach, area] + part[far, area]
        copy = hop(way, 1, way)
        copy.start()
        sends.append(copy)
    for step in range(2, reach + 1):
        for way in range(2):
            sign = 1 - 2 * way
            offset = sign * (reach - step + 1)
            arrived[offset].wait_recv()
        for turn in range(PIECES):
            for way in range(2):
                sign = 1 - 2 * way
                offset = sign * (reach - step + 1)
                piece = (1 - way if turn == 0 else way) if step == 2 else (1 - way if turn == 0 else way)
                area = pl.ds(piece * rows, rows)
                own = mate[offset % chips, area] + part[member(offset, core), area]
                if step > 2 or piece == way:
                    hop(way, step - 1, piece).wait_recv()
                    own = own + held[way, step - 2, area]
                held[way, step - 2, area] = own
                copy = hop(way, step, piece)
                copy.start()
                sends.append(copy)
    arrived[0].wait_recv()
    for way in range(2):
        for piece in range(PIECES):
            hop(way, reach, piece).wait_recv()
    hours = hour_out.shape[0]
    total = mate[0] + part[me] + held[0, reach - 1] + held[1, reach - 1]
    hour_out[...] = total[:hours] * scale
    block_out[...] = total[hours:] * scale
    for copy in sends:
        copy.wait_send()
    for copy in swaps:
        copy.wait_send()


def scatter(devices, scale, part, hours, blocks):
    reach = devices // 4
    chips = devices // 2
    rows, width = part.shape[1:]
    sems = (2, reach, PIECES)
    return pl.pallas_call(
        functools.partial(scatter_kernel, devices, scale),
        out_shape=[
            jax.ShapeDtypeStruct((hours, width), jnp.float32),
            jax.ShapeDtypeStruct((blocks, width), jnp.float32),
        ],
        in_specs=[pl.BlockSpec(memory_space=pltpu.VMEM)],
        out_specs=[pl.BlockSpec(memory_space=pltpu.VMEM)] * 2,
        scratch_shapes=[
            pltpu.VMEM((chips, rows, width), jnp.float32),
            pltpu.VMEM((2, reach, rows, width), jnp.float32),
            pltpu.SemaphoreType.DMA(sems),
            pltpu.SemaphoreType.DMA(sems),
            pltpu.SemaphoreType.DMA((chips,)),
            pltpu.SemaphoreType.DMA((chips,)),
        ],
        compiler_params=pltpu.CompilerParams(
            collective_id=1, has_side_effects=True, vmem_limit_bytes=56 * 2**20
        ),
        name="scatter_sums",
    )(part)


def tile_kernel(slots, hours, scale, info, total, rows_ref, list_ref, port_ref, part, port_grad):
    side = rows_ref.shape[1] - hours
    width = rows_ref.shape[2]
    entries = list_ref.shape[2]
    per_hour = hours // side
    part[...] = jnp.zeros_like(part)
    port_grad[...] = jnp.zeros_like(port_grad)
    down = lax.broadcasted_iota(jnp.int32, (side, entries), 0)
    along = lax.broadcasted_iota(jnp.int32, (entries, side), 1)

    def visit(step, carry):
        code = info[step]
        flat = code & 0xFFFF
        hour = (code >> 16) & 0xFF
        port = code >> 24
        owner = flat // slots
        slot = flat % slots
        hour_owner = hour // per_hour
        hour_rows = pl.ds(pl.multiple_of((hour % per_hour) * side, side), side)
        port_rows = pl.ds(pl.multiple_of(port * side, side), side)
        first = list_ref[owner, pl.ds(slot, 1), :]
        second = list_ref[owner, pl.ds(slots + slot, 1), :]
        packed = (
            (first & 127)
            + ((first >> 16) << 7)
            + ((second & 127) << 14)
            + ((second >> 16) << 21)
        )
        wide = jnp.broadcast_to(packed, (side, entries))
        tall = wide.T
        put_a = (down == (wide & 127)).astype(jnp.bfloat16)
        put_b = (down == ((wide >> 7) & 127)).astype(jnp.bfloat16)
        put_c = (down == ((wide >> 14) & 127)).astype(jnp.bfloat16)
        pick_a = (along == (tall & 127)).astype(jnp.bfloat16)
        pick_b = (along == ((tall >> 7) & 127)).astype(jnp.bfloat16)
        pick_c = (along == ((tall >> 14) & 127)).astype(jnp.bfloat16)
        counts = (tall >> 21)[:, :1].astype(jnp.float32)
        block_a = rows_ref[owner, pl.ds(hours, side), :]
        block_b = rows_ref[hour_owner, hour_rows, :]
        block_c = port_ref[port_rows, :]
        dot = functools.partial(jnp.dot, preferred_element_type=jnp.float32)
        rows_a = dot(pick_a, block_a)
        rows_b = dot(pick_b, block_b)
        rows_c = dot(pick_c, block_c)
        model = jnp.sum(rows_a * rows_b * rows_c, axis=1, keepdims=True)
        ratio = counts / model
        scaled_a = ratio * rows_a
        scaled_b = ratio * rows_b
        back_a = dot(put_a, (scaled_b * rows_c).astype(jnp.bfloat16))
        back_b = dot(put_b, (scaled_a * rows_c).astype(jnp.bfloat16))
        back_c = dot(put_c, (scaled_a * rows_b).astype(jnp.bfloat16))
        sum_a = jnp.sum(block_a.astype(jnp.float32), axis=0, keepdims=True)
        sum_b = jnp.sum(block_b.astype(jnp.float32), axis=0, keepdims=True)
        sum_c = jnp.sum(block_c.astype(jnp.float32), axis=0, keepdims=True)
        part[owner, pl.ds(hours, side), :] += sum_b * sum_c - back_a
        part[hour_owner, hour_rows, :] += sum_a * sum_c - back_b
        port_grad[port_rows, :] += (sum_a * sum_b - back_c) * scale
        return carry

    lax.fori_loop(0, total[0], visit, 0)


def tiles(slots, hours, scale, info, total, rows, lists, port_factor):
    devices = rows.shape[0]
    vmem = pl.BlockSpec(memory_space=pltpu.VMEM)
    smem = pl.BlockSpec(memory_space=pltpu.SMEM)
    return pl.pallas_call(
        functools.partial(tile_kernel, slots, hours, scale),
        out_shape=[
            jax.ShapeDtypeStruct(rows.shape, jnp.float32),
            jax.ShapeDtypeStruct(port_factor.shape, jnp.float32),
        ],
        in_specs=[smem, smem, vmem, vmem, vmem],
        out_specs=[vmem, vmem],
        compiler_params=pltpu.CompilerParams(vmem_limit_bytes=56 * 2**20),
        name="tile_terms",
    )(info, total, rows, lists, port_factor)


def local(
    block_factor,
    hour_factor,
    port_factor,
    tile_count,
    hour_tiles,
    port_tiles,
    entry_coords,
    entry_counts,
):
    devices = lax.axis_size("block")
    side = block_factor.shape[0]
    hours = hour_factor.shape[0]
    slots = hour_tiles.shape[0]
    entries = entry_counts.shape[1]
    port_local = port_factor.shape[0] // side
    per_peer = (slots + devices - 1) // devices
    capacity = devices * per_peer

    first = entry_coords[:, 0] + (entry_coords[:, 1] << 16)
    second = entry_coords[:, 2] + (entry_counts << 16)
    meta = jnp.stack([hour_tiles, port_tiles, jnp.broadcast_to(tile_count, (slots,))])
    meta = jnp.pad(meta, ((0, 13), (0, entries - slots)))
    rows, lists = gather(
        devices,
        jnp.concatenate([hour_factor, block_factor]),
        jnp.concatenate([first, second, meta]),
    )

    hour_of = lists[:, 2 * slots, :slots]
    port_of = lists[:, 2 * slots + 1, :slots]
    live = jnp.arange(slots, dtype=jnp.int32)[None, :] < lists[:, 2 * slots + 2, :1]
    mine = (live & (port_of // port_local == lax.axis_index("block"))).reshape(-1)
    order = jnp.arange(devices * slots, dtype=jnp.int32)
    code = order + (hour_of.reshape(-1) << 16) + ((port_of % port_local).reshape(-1) << 24)
    before = jnp.sum(
        ((order[None, :] < order[:, None]) & mine[None, :]).astype(jnp.int32), axis=1
    )
    spot = jnp.where(mine, before, capacity)
    hits = spot[None, :] == jnp.arange(capacity, dtype=jnp.int32)[:, None]
    info = jnp.sum(jnp.where(hits, code[None, :], 0), axis=1)
    total = jnp.sum(mine.astype(jnp.int32)).reshape(1)

    scale = 1.0 / side
    part, port_grad = tiles(slots, hours, scale, info, total, rows, lists, port_factor)
    hour_grad, block_grad = scatter(devices, scale, part, hours, side)
    return (block_grad, hour_grad, port_grad)


def solution(mesh):
    row = P(("group", "block"), None)
    one = P(("group", "block"))
    in_specs = (row, row, row, one, one, one, P(("group", "block"), None, None), row)
    return jax.shard_map(
        local, mesh=mesh, in_specs=in_specs, out_specs=(row, row, row), check_vma=False
    )
```

time: 585 us -> 163 us (0.28)
  the two profiles are of different devices: /device:TPU:19 before, /device:TPU:0 now
where the time goes in v1:
time: 163 us
  Pallas kernels  149 us (91%)
  other arithmetic  7.56 us (5%)
  local copies, waits for them, and re-layouts  4.95 us (3%)
    pallas_call x1, Pallas kernels, scatter(): pl.pallas_call(functools.partial(scatter_kernel, devices, scale), out_sha...  62.3 us
    pallas_call x1, Pallas kernels, gather(): pl.pallas_call(functools.partial(gather_kernel, devices), out_shape=[jax....  43.7 us
    pallas_call x1, Pallas kernels, tiles(): pl.pallas_call(functools.partial(tile_kernel, slots, hours, scale), out_s...  43.1 us
    unnamed x2, local copies, waits for them, and re-layouts  3.44 us

profile of v1, /device:TPU:0, one launch (start us, length us, event | category | flops | bytes accessed | tf_op | source)
XLA Modules:
  0.0 162.9 jit_solution(17948967137732305837)
XLA Ops:
  1.3 0.1 pad.10.clone
  1.4 0.7 add_add_fusion
  2.1 0.9 bitcast_add_fusion
  3.0 0.9 add_bitcast_fusion
  3.9 0.7 pad_add_fusion.refs_1_
  4.5 1.7 %pad_maximum_fusion.refs_0_ = bf16[640,256]{1,0:T(8,128)(2,1)} fusion(bf16[128,256]{1,0:T(8,128)(2,1)} %param.8, bf16[512,256]{1,0:T(8,128)(2,1)} %param.9), kind=kLoop, calls=%fused_computation.3 | loop fusion | flops 655360 | bytes 655360 | tf_op jit(solution)/shard_map/concatenate | solution.py:375
  6.3 43.7 %gather_rows.1 = (bf16[16,640,256]{2,1,0:T(8,128)(2,1)}, s32[16,144,256]{2,1,0:T(8,128)}) custom-call(bf16[640,256]{1,0:T(8,128)(2,1)} %pad_maximum_fusion.refs_0_, s32[144,256]{1,0:T(8,128)} %pad_add_fusion.refs_1_), custom_call_target="tpu_custom_call" | custom-call | tf_op jit(solution)/shard_map/gather_rows/pallas_call | solution.py:141
  50.0 1.2 slice_reduce_fusion
  51.2 0.1 iota_compare_fusion.2
  51.2 0.1 lt.50
  51.3 1.0 slice_reduce_fusion.1
  52.3 0.7 convert_reduce_fusion.1
  53.0 0.1 squeeze.12
  53.1 0.2 convert_reduce_fusion
  53.3 0.1 shift_left.34
  53.4 0.6 select_reduce_fusion.info
  54.1 43.1 %tile_terms.1 = (f32[16,640,256]{2,1,0:T(8,128)}, f32[4096,256]{1,0:T(8,128)}) custom-call(s32[64]{0:T(128)} %select_reduce_fusion.info, s32[1]{0:T(128)} %bitcast.6.total, bf16[16,640,256]{2,1,0:T(8,128)(2,1)} %get-tuple-element.10.rows_ref, s32[16,144,256]{2,1,0:T(8,128)} %get-tuple-element.9.list_ref, bf16[4096,256]{1,0:T(8,128)(2,1)} %port_ref.1), custom_call_target="tpu_custom_call" | custom-call | tf_op jit(solution)/shard_map/tile_terms/pallas_call | solution.py:337
  97.1 62.3 %scatter_sums.1 = (f32[512,256]{1,0:T(8,128)}, f32[128,256]{1,0:T(8,128)}) custom-call(f32[16,640,256]{2,1,0:T(8,128)} %get-tuple-element.11.part), custom_call_target="tpu_custom_call" | custom-call | tf_op jit(solution)/shard_map/scatter_sums/pallas_call | solution.py:248
  159.4 1.6 copy.14
  161.0 1.9 %copy.15 = f32[512,256]{1,0:T(8,128)} copy(f32[512,256]{1,0:T(8,128)} %get-tuple-element.24) | data formatting | bytes 1048576
  (2 shorter events, 0.0 us)

commit v2 on v1

--- a/solution.py
+++ b/solution.py
@@ -9,6 +9,7 @@
 
 MESH = pl.DeviceIdType.MESH
 PIECES = 2
+TOGETHER = 2
 
 
 def ring(devices):
@@ -37,30 +38,80 @@
     pl.semaphore_wait(barrier, len(partners))
 
 
-def gather_kernel(devices, *refs):
-    count = (len(refs) - 7) // 2
-    ins, outs = refs[:count], refs[count : 2 * count]
-    local_sem, send_sem, recv_sem, pair_send, pair_recv, own_send, own_recv = refs[2 * count :]
+def file_kernel(port_local, per_peer, tile_count, hour_tiles, port_tiles, coords, counts, box, code, used):
+    devices = box.shape[0]
+    box[...] = jnp.zeros_like(box)
+    code[...] = jnp.full_like(code, -1)
+
+    def clear(owner, carry):
+        used[owner] = 0
+        return carry
+
+    def visit(slot, carry):
+        port = port_tiles[slot]
+        owner = port // port_local
+        spot = used[owner]
+        used[owner] = spot + 1
+        word = (hour_tiles[slot] << 16) + port % port_local
+        code[owner, pl.ds(spot, 1), :] = jnp.full((1, code.shape[2]), word, jnp.int32)
+        at = coords[slot]
+        box[owner, pl.ds(2 * spot, 1), :] = at[0:1] + (at[1:2] << 16)
+        box[owner, pl.ds(2 * spot + 1, 1), :] = at[2:3] + (counts[pl.ds(slot, 1), :] << 16)
+        return carry
+
+    lax.fori_loop(0, devices, clear, 0)
+    lax.fori_loop(0, tile_count[0], visit, 0)
+
+
+def file_lists(devices, port_local, per_peer, tile_count, hour_tiles, port_tiles, coords, counts):
+    entries = counts.shape[1]
+    vmem = pl.BlockSpec(memory_space=pltpu.VMEM)
+    smem = pl.BlockSpec(memory_space=pltpu.SMEM)
+    return pl.pallas_call(
+        functools.partial(file_kernel, port_local, per_peer),
+        out_shape=[
+            jax.ShapeDtypeStruct((devices, (2 * per_peer + 7) // 8 * 8, entries), jnp.int32),
+            jax.ShapeDtypeStruct((devices, (per_peer + 7) // 8 * 8, 128), jnp.int32),
+        ],
+        in_specs=[smem, smem, smem, vmem, vmem],
+        out_specs=[vmem, vmem],
+        scratch_shapes=[pltpu.SMEM((devices,), jnp.int32)],
+        name="file_lists",
+    )(tile_count, hour_tiles, port_tiles, coords, counts)
+
+
+def gather_kernel(devices, hour, block, box, code, rows_out, box_out, code_out, *sems):
+    (local_sem, send_sem, recv_sem, pair_send, pair_recv, own_send, own_recv, list_send, list_recv) = sems
+    ins = (hour, block)
+    count = len(ins)
+    base = (0, hour.shape[0])
     reach = devices // 4
     group, me, core, member = ring(devices)
     sibling = member(0, 1 - core)
-    greet(group, (member(-1, core), member(1, core), sibling))
+    others = [lax.rem(me + shift, devices) for shift in range(1, devices)]
+    greet(group, others)
+
+    def area(a, piece):
+        rows = ins[a].shape[0] // PIECES
+        return pl.ds(base[a] + piece * rows, rows)
 
     started = []
     for a in range(count):
-        keep = pltpu.make_async_copy(ins[a], outs[a].at[me], local_sem.at[a])
-        keep.start()
+        keep = pltpu.make_async_copy(
+            ins[a], rows_out.at[me, pl.ds(base[a], ins[a].shape[0])], local_sem.at[a]
+        )
         started.append(keep)
+    started.append(pltpu.make_async_copy(box.at[me], box_out.at[me], local_sem.at[count]))
+    started.append(pltpu.make_async_copy(code.at[me], code_out.at[me], local_sem.at[count + 1]))
 
     def hop(a, way, step, piece):
         rows = ins[a].shape[0] // PIECES
         sign = 1 - 2 * way
         origin = member(-sign * (step - 1), core)
-        part = pl.ds(piece * rows, rows)
-        here = ins[a].at[part] if step == 1 else outs[a].at[origin, part]
+        there = rows_out.at[origin, area(a, piece)]
         return pltpu.make_async_remote_copy(
-            src_ref=here,
-            dst_ref=outs[a].at[origin, part],
+            src_ref=ins[a].at[pl.ds(piece * rows, rows)] if step == 1 else there,
+            dst_ref=there,
             send_sem=send_sem.at[a, way, step - 1, piece],
             recv_sem=recv_sem.at[a, way, step - 1, piece],
             device_id=(group, member(sign, core)),
@@ -68,13 +119,11 @@
         )
 
     def share(a, way, step, piece, lane):
-        rows = ins[a].shape[0] // PIECES
         sign = 1 - 2 * way
-        origin = member(-sign * step, lane)
-        part = pl.ds(piece * rows, rows)
+        there = rows_out.at[member(-sign * step, lane), area(a, piece)]
         return pltpu.make_async_remote_copy(
-            src_ref=outs[a].at[origin, part],
-            dst_ref=outs[a].at[origin, part],
+            src_ref=there,
+            dst_ref=there,
             send_sem=pair_send.at[a, way, step - 1, piece],
             recv_sem=pair_recv.at[a, way, step - 1, piece],
             device_id=(group, sibling),
@@ -84,7 +133,7 @@
     def own_share(a):
         return pltpu.make_async_remote_copy(
             src_ref=ins[a],
-            dst_ref=outs[a].at[me],
+            dst_ref=rows_out.at[me, pl.ds(base[a], ins[a].shape[0])],
             send_sem=own_send.at[a],
             recv_sem=own_recv.at[a],
             device_id=(group, sibling),
@@ -106,10 +155,25 @@
             copy = hop(a, way, 1, piece)
             copy.start()
             sends.append(copy)
+    lists = []
+    for shift, other in enumerate(others):
+        for kind, (here, there) in enumerate(((box, box_out), (code, code_out))):
+            copy = pltpu.make_async_remote_copy(
+                src_ref=here.at[other],
+                dst_ref=there.at[me],
+                send_sem=list_send.at[kind, shift],
+                recv_sem=list_recv.at[kind, shift],
+                device_id=(group, other),
+                device_id_type=MESH,
+            )
+            copy.start()
+            lists.append(copy)
     for a in range(count):
         copy = own_share(a)
         copy.start()
         sends.append(copy)
+    for keep in started:
+        keep.start()
     for step in range(1, reach + 1):
         onward = plan(step + 1) if step < reach else []
         for way, piece in plan(step):
@@ -122,39 +186,48 @@
                 copy = share(a, way, step, piece, core)
                 copy.start()
                 sends.append(copy)
+    for copy in lists:
+        copy.wait_recv()
     for a in range(count):
         own_share(a).wait_recv()
     for step in range(1, reach + 1):
         for way, piece in plan(step):
             for a in range(count):
                 share(a, way, step, piece, 1 - core).wait_recv()
-    for copy in sends:
+    for copy in sends + lists:
         copy.wait_send()
     for copy in started:
         copy.wait()
 
 
-def gather(devices, *arrays):
+def gather(devices, hour, block, box, code):
     reach = devices // 4
-    count = len(arrays)
+    count = 2
     sems = (count, 2, reach, PIECES)
+    rows = hour.shape[0] + block.shape[0]
     return pl.pallas_call(
         functools.partial(gather_kernel, devices),
-        out_shape=[jax.ShapeDtypeStruct((devices,) + x.shape, x.dtype) for x in arrays],
-        in_specs=[pl.BlockSpec(memory_space=pl.ANY)] * count,
-        out_specs=[pl.BlockSpec(memory_space=pl.ANY)] * count,
+        out_shape=[
+            jax.ShapeDtypeStruct((devices, rows, hour.shape[1]), hour.dtype),
+            jax.ShapeDtypeStruct(box.shape, box.dtype),
+            jax.ShapeDtypeStruct(code.shape, code.dtype),
+        ],
+        in_specs=[pl.BlockSpec(memory_space=pl.ANY)] * 4,
+        out_specs=[pl.BlockSpec(memory_space=pl.ANY)] * 3,
         scratch_shapes=[
-            pltpu.SemaphoreType.DMA((count,)),
+            pltpu.SemaphoreType.DMA((count + 2,)),
             pltpu.SemaphoreType.DMA(sems),
             pltpu.SemaphoreType.DMA(sems),
             pltpu.SemaphoreType.DMA(sems),
             pltpu.SemaphoreType.DMA(sems),
             pltpu.SemaphoreType.DMA((count,)),
             pltpu.SemaphoreType.DMA((count,)),
+            pltpu.SemaphoreType.DMA((2, devices - 1)),
+            pltpu.SemaphoreType.DMA((2, devices - 1)),
         ],
         compiler_params=pltpu.CompilerParams(collective_id=0, has_side_effects=True),
         name="gather_rows",
-    )(*arrays)
+    )(hour, block, box, code)
 
 
 def scatter_kernel(devices, scale, part, hour_out, block_out, mate, held, *sems):
@@ -268,28 +341,36 @@
     )(part)
 
 
-def tile_kernel(slots, hours, scale, info, total, rows_ref, list_ref, port_ref, part, port_grad):
+def tile_kernel(per_peer, hours, scale, codes, rows_ref, box_ref, port_ref, part, port_grad, kept):
     side = rows_ref.shape[1] - hours
-    width = rows_ref.shape[2]
-    entries = list_ref.shape[2]
+    entries = box_ref.shape[2]
     per_hour = hours // side
+    spots = codes.shape[0]
+
+    def keep(spot, count):
+        kept[count] = spot
+        return count + (codes[spot] >= 0).astype(jnp.int32)
+
+    total = lax.fori_loop(0, spots, keep, 0)
     part[...] = jnp.zeros_like(part)
     port_grad[...] = jnp.zeros_like(port_grad)
     down = lax.broadcasted_iota(jnp.int32, (side, entries), 0)
     along = lax.broadcasted_iota(jnp.int32, (entries, side), 1)
-
-    def visit(step, carry):
-        code = info[step]
-        flat = code & 0xFFFF
-        hour = (code >> 16) & 0xFF
-        port = code >> 24
-        owner = flat // slots
-        slot = flat % slots
+    dot = functools.partial(jnp.dot, preferred_element_type=jnp.float32)
+
+    def terms(index):
+        here = index < total
+        spot = kept[jnp.minimum(index, total - 1)]
+        code = codes[spot]
+        hour = code >> 16
+        port = code & 0xFFFF
+        owner = spot // per_peer
+        line = 2 * (spot % per_peer)
         hour_owner = hour // per_hour
         hour_rows = pl.ds(pl.multiple_of((hour % per_hour) * side, side), side)
         port_rows = pl.ds(pl.multiple_of(port * side, side), side)
-        first = list_ref[owner, pl.ds(slot, 1), :]
-        second = list_ref[owner, pl.ds(slots + slot, 1), :]
+        first = box_ref[owner, pl.ds(line, 1), :]
+        second = box_ref[owner, pl.ds(line + 1, 1), :]
         packed = (
             (first & 127)
             + ((first >> 16) << 7)
@@ -308,43 +389,51 @@
         block_a = rows_ref[owner, pl.ds(hours, side), :]
         block_b = rows_ref[hour_owner, hour_rows, :]
         block_c = port_ref[port_rows, :]
-        dot = functools.partial(jnp.dot, preferred_element_type=jnp.float32)
         rows_a = dot(pick_a, block_a)
         rows_b = dot(pick_b, block_b)
         rows_c = dot(pick_c, block_c)
         model = jnp.sum(rows_a * rows_b * rows_c, axis=1, keepdims=True)
-        ratio = counts / model
+        ratio = jnp.where(here, counts / model, 0.0)
         scaled_a = ratio * rows_a
         scaled_b = ratio * rows_b
         back_a = dot(put_a, (scaled_b * rows_c).astype(jnp.bfloat16))
         back_b = dot(put_b, (scaled_a * rows_c).astype(jnp.bfloat16))
         back_c = dot(put_c, (scaled_a * rows_b).astype(jnp.bfloat16))
+        live = jnp.where(here, 1.0, 0.0)
         sum_a = jnp.sum(block_a.astype(jnp.float32), axis=0, keepdims=True)
         sum_b = jnp.sum(block_b.astype(jnp.float32), axis=0, keepdims=True)
         sum_c = jnp.sum(block_c.astype(jnp.float32), axis=0, keepdims=True)
-        part[owner, pl.ds(hours, side), :] += sum_b * sum_c - back_a
-        part[hour_owner, hour_rows, :] += sum_a * sum_c - back_b
-        port_grad[port_rows, :] += (sum_a * sum_b - back_c) * scale
+        part_a = live * (sum_b * sum_c) - back_a
+        part_b = live * (sum_a * sum_c) - back_b
+        part_c = (live * (sum_a * sum_b) - back_c) * scale
+        return owner, hour_owner, hour_rows, port_rows, part_a, part_b, part_c
+
+    def visit(step, carry):
+        done = [terms(TOGETHER * step + turn) for turn in range(TOGETHER)]
+        for owner, hour_owner, hour_rows, port_rows, part_a, part_b, part_c in done:
+            part[owner, pl.ds(hours, side), :] += part_a
+            part[hour_owner, hour_rows, :] += part_b
+            port_grad[port_rows, :] += part_c
         return carry
 
-    lax.fori_loop(0, total[0], visit, 0)
-
-
-def tiles(slots, hours, scale, info, total, rows, lists, port_factor):
-    devices = rows.shape[0]
+    lax.fori_loop(0, (total + TOGETHER - 1) // TOGETHER, visit, 0)
+
+
+def tiles(per_peer, hours, scale, codes, rows, box, port_factor):
     vmem = pl.BlockSpec(memory_space=pltpu.VMEM)
     smem = pl.BlockSpec(memory_space=pltpu.SMEM)
     return pl.pallas_call(
-        functools.partial(tile_kernel, slots, hours, scale),
+        functools.partial(tile_kernel, per_peer, hours, scale),
         out_shape=[
             jax.ShapeDtypeStruct(rows.shape, jnp.float32),
             jax.ShapeDtypeStruct(port_factor.shape, jnp.float32),
         ],
-        in_specs=[smem, smem, vmem, vmem, vmem],
+        in_specs=[smem, vmem, vmem, vmem],
         out_specs=[vmem, vmem],
+        scratch_shapes=[pltpu.SMEM((codes.shape[0] + 1,), jnp.int32)],
         compiler_params=pltpu.CompilerParams(vmem_limit_bytes=56 * 2**20),
         name="tile_terms",
-    )(info, total, rows, lists, port_factor)
+    )(codes, rows, box, port_factor)
 
 
 def local(
@@ -361,37 +450,17 @@
     side = block_factor.shape[0]
     hours = hour_factor.shape[0]
     slots = hour_tiles.shape[0]
-    entries = entry_counts.shape[1]
     port_local = port_factor.shape[0] // side
     per_peer = (slots + devices - 1) // devices
-    capacity = devices * per_peer
-
-    first = entry_coords[:, 0] + (entry_coords[:, 1] << 16)
-    second = entry_coords[:, 2] + (entry_counts << 16)
-    meta = jnp.stack([hour_tiles, port_tiles, jnp.broadcast_to(tile_count, (slots,))])
-    meta = jnp.pad(meta, ((0, 13), (0, entries - slots)))
-    rows, lists = gather(
-        devices,
-        jnp.concatenate([hour_factor, block_factor]),
-        jnp.concatenate([first, second, meta]),
+
+    box, code = file_lists(
+        devices, port_local, per_peer, tile_count, hour_tiles, port_tiles, entry_coords, entry_counts
     )
-
-    hour_of = lists[:, 2 * slots, :slots]
-    port_of = lists[:, 2 * slots + 1, :slots]
-    live = jnp.arange(slots, dtype=jnp.int32)[None, :] < lists[:, 2 * slots + 2, :1]
-    mine = (live & (port_of // port_local == lax.axis_index("block"))).reshape(-1)
-    order = jnp.arange(devices * slots, dtype=jnp.int32)
-    code = order + (hour_of.reshape(-1) << 16) + ((port_of % port_local).reshape(-1) << 24)
-    before = jnp.sum(
-        ((order[None, :] < order[:, None]) & mine[None, :]).astype(jnp.int32), axis=1
-    )
-    spot = jnp.where(mine, before, capacity)
-    hits = spot[None, :] == jnp.arange(capacity, dtype=jnp.int32)[:, None]
-    info = jnp.sum(jnp.where(hits, code[None, :], 0), axis=1)
-    total = jnp.sum(mine.astype(jnp.int32)).reshape(1)
+    rows, box, code = gather(devices, hour_factor, block_factor, box, code)
+    codes = code[:, :per_peer, 0].reshape(-1)
 
     scale = 1.0 / side
-    part, port_grad = tiles(slots, hours, scale, info, total, rows, lists, port_factor)
+    part, port_grad = tiles(per_peer, hours, scale, codes, rows, box, port_factor)
     hour_grad, block_grad = scatter(devices, scale, part, hours, side)
     return (block_grad, hour_grad, port_grad)
 

time: 163 us -> 151 us (0.926)
  other arithmetic: 7.56 us -> 0 us
  Pallas kernels: 149 us -> 143 us
  local copies, waits for them, and re-layouts: 4.95 us -> 6.99 us
    pallas_call x1, Pallas kernels: 43.7 us -> 38.7 us  [gather(): pl.pallas_call(functools.partial(gather_kernel, devices), out_shape=[jax....]
    concatenate x2 -> x0, other arithmetic: 2.41 us -> none  [the longest x1 1.73 us: local(): jnp.concatenate([hour_factor, block_factor])]
    add x3 -> x0, other arithmetic: 1.78 us -> none  [the longest x1 0.88 us: local(): first = entry_coords[:, 0] + (entry_coords[:, 1] << 16)]
    unnamed x2 -> x3, local copies, waits for them, and re-layouts: 3.44 us -> 5.2 us
    pallas_call x1 -> x2, Pallas kernels: 43.1 us -> 42.2 us  [the longest x1 39.4 us: tiles(): pl.pallas_call(functools.partial(tile_kernel, per_peer, hours, scale), ou...]
where the time goes in v2:
time: 151 us
  Pallas kernels  143 us (95%)
  local copies, waits for them, and re-layouts  6.99 us (5%)
    pallas_call x1, Pallas kernels, scatter(): pl.pallas_call(functools.partial(scatter_kernel, devices, scale), out_sha...  62.1 us
    pallas_call x1, Pallas kernels, tiles(): pl.pallas_call(functools.partial(tile_kernel, per_peer, hours, scale), ou...  39.4 us
    pallas_call x1, Pallas kernels, gather(): pl.pallas_call(functools.partial(gather_kernel, devices), out_shape=[jax....  38.7 us
    unnamed x3, local copies, waits for them, and re-layouts  5.2 us

profile of v2, /device:TPU:0, one launch (start us, length us, event | category | flops | bytes accessed | tf_op | source)
XLA Modules:
  0.0 151.3 jit_solution(2038928454194738277)
XLA Ops:
  1.3 1.8 %copy.12.coords = s32[64,3,256]{2,1,0:T(4,128)} copy(s32[64,3,256]{2,0,1:T(8,128)} %param.14) | data formatting | bytes 393216 | tf_op args[6]
  3.0 2.9 %file_lists.1 = (s32[16,8,256]{2,1,0:T(8,128)}, s32[16,8,128]{2,1,0:T(8,128)}) custom-call(s32[1]{0:T(128)S(6)} %copy.15.tile_count, s32[64]{0:T(128)} %hour_tiles.1, s32[64]{0:T(128)} %port_tiles.1, s32[64,3,256]{2,1,0:T(4,128)} %copy.12.coords, s32[64,256]{1,0:T(8,128)} %counts.1), custom_call_target="tpu_custom_call" | custom-call | tf_op jit(solution)/shard_map/file_lists/pallas_call | solution.py:70
  5.9 38.7 %gather_rows.1 = (bf16[16,640,256]{2,1,0:T(8,128)(2,1)}, s32[16,8,256]{2,1,0:T(8,128)}, s32[16,8,128]{2,1,0:T(8,128)}) custom-call(bf16[512,256]{1,0:T(8,128)(2,1)} %hour.1, bf16[128,256]{1,0:T(8,128)(2,1)} %block.1, s32[16,8,256]{2,1,0:T(8,128)} %get-tuple-element.12.box, s32[16,8,128]{2,1,0:T(8,128)} %get-tuple-element.13.code), custom_call_target="tpu_custom_call" | custom-call | tf_op jit(solution)/shard_map/gather_rows/pallas_call | solution.py:208
  44.6 1.2 slice_reduce_fusion
  45.8 0.6 reshape_squeeze.3.codes
  46.4 39.4 %tile_terms.1 = (f32[16,640,256]{2,1,0:T(8,128)}, f32[4096,256]{1,0:T(8,128)}) custom-call(s32[64]{0:T(128)} %reshape_squeeze.3.codes, bf16[16,640,256]{2,1,0:T(8,128)(2,1)} %get-tuple-element.15.rows_ref, s32[16,8,256]{2,1,0:T(8,128)} %get-tuple-element.16.box_ref, bf16[4096,256]{1,0:T(8,128)(2,1)} %port_ref.1), custom_call_target="tpu_custom_call" | custom-call | tf_op jit(solution)/shard_map/tile_terms/pallas_call | solution.py:425
  85.8 62.1 %scatter_sums.1 = (f32[512,256]{1,0:T(8,128)}, f32[128,256]{1,0:T(8,128)}) custom-call(f32[16,640,256]{2,1,0:T(8,128)} %get-tuple-element.17.part), custom_call_target="tpu_custom_call" | custom-call | tf_op jit(solution)/shard_map/scatter_sums/pallas_call | solution.py:321
  147.9 1.6 %copy.16 = f32[128,256]{1,0:T(8,128)} copy(f32[128,256]{1,0:T(8,128)} %get-tuple-element.24) | data formatting | bytes 262144
  149.5 1.9 %copy.17 = f32[512,256]{1,0:T(8,128)} copy(f32[512,256]{1,0:T(8,128)} %get-tuple-element.25) | data formatting | bytes 1048576

commit v3 on v2

--- a/solution.py
+++ b/solution.py
@@ -335,7 +335,7 @@
             pltpu.SemaphoreType.DMA((chips,)),
         ],
         compiler_params=pltpu.CompilerParams(
-            collective_id=1, has_side_effects=True, vmem_limit_bytes=56 * 2**20
+            collective_id=1, has_side_effects=True, vmem_limit_bytes=part.size * 4 + 8 * 2**20
         ),
         name="scatter_sums",
     )(part)
@@ -379,12 +379,12 @@
         )
         wide = jnp.broadcast_to(packed, (side, entries))
         tall = wide.T
-        put_a = (down == (wide & 127)).astype(jnp.bfloat16)
-        put_b = (down == ((wide >> 7) & 127)).astype(jnp.bfloat16)
-        put_c = (down == ((wide >> 14) & 127)).astype(jnp.bfloat16)
+        put_a = (down == (first & 127)).astype(jnp.bfloat16)
+        put_b = (down == (first >> 16)).astype(jnp.bfloat16)
+        put_c = (down == (second & 127)).astype(jnp.bfloat16)
         pick_a = (along == (tall & 127)).astype(jnp.bfloat16)
-        pick_b = (along == ((tall >> 7) & 127)).astype(jnp.bfloat16)
-        pick_c = (along == ((tall >> 14) & 127)).astype(jnp.bfloat16)
+        pick_b = ((along << 7) == (tall & (127 << 7))).astype(jnp.bfloat16)
+        pick_c = ((along << 14) == (tall & (127 << 14))).astype(jnp.bfloat16)
         counts = (tall >> 21)[:, :1].astype(jnp.float32)
         block_a = rows_ref[owner, pl.ds(hours, side), :]
         block_b = rows_ref[hour_owner, hour_rows, :]
@@ -425,13 +425,15 @@
     return pl.pallas_call(
         functools.partial(tile_kernel, per_peer, hours, scale),
         out_shape=[
-            jax.ShapeDtypeStruct(rows.shape, jnp.float32),
+            pltpu.VMEM(rows.shape, jnp.float32),
             jax.ShapeDtypeStruct(port_factor.shape, jnp.float32),
         ],
         in_specs=[smem, vmem, vmem, vmem],
         out_specs=[vmem, vmem],
         scratch_shapes=[pltpu.SMEM((codes.shape[0] + 1,), jnp.int32)],
-        compiler_params=pltpu.CompilerParams(vmem_limit_bytes=56 * 2**20),
+        compiler_params=pltpu.CompilerParams(
+            vmem_limit_bytes=rows.size * 2 + port_factor.size * 6 + 8 * 2**20
+        ),
         name="tile_terms",
     )(codes, rows, box, port_factor)
 

time: 151 us -> 142 us (0.940); the launches traced: 151 us -> 141 us
  Pallas kernels: 143 us -> 130 us
  local copies, waits for them, and re-layouts: 6.99 us -> 9.47 us
    pallas_call x1, Pallas kernels: 62.1 us -> 54.8 us  [scatter(): pl.pallas_call(functools.partial(scatter_kernel, devices, scale), out_sha...]
    pallas_call x1, Pallas kernels: 39.4 us -> 33.3 us  [tiles(): pl.pallas_call(functools.partial(tile_kernel, per_peer, hours, scale), ou...]
    unnamed x3 -> x9, local copies, waits for them, and re-layouts: 5.2 us -> 8.19 us
where the time goes in v3:
time: 142 us; the launch traced here: 141 us
  Pallas kernels  130 us (92%)
  local copies, waits for them, and re-layouts  9.47 us (7%)
    pallas_call x1, Pallas kernels, scatter(): pl.pallas_call(functools.partial(scatter_kernel, devices, scale), out_sha...  54.8 us
    pallas_call x1, Pallas kernels, gather(): pl.pallas_call(functools.partial(gather_kernel, devices), out_shape=[jax....  39.2 us
    pallas_call x1, Pallas kernels, tiles(): pl.pallas_call(functools.partial(tile_kernel, per_peer, hours, scale), ou...  33.3 us
    unnamed x9, local copies, waits for them, and re-layouts  8.19 us

profile of v3, /device:TPU:0, one launch (start us, length us, event | category | flops | bytes accessed | tf_op | source)
XLA Modules:
  0.0 140.6 jit_solution(934626472763382848)
XLA Ops:
  1.3 1.8 %copy.12.coords = s32[64,3,256]{2,1,0:T(4,128)} copy(s32[64,3,256]{2,0,1:T(8,128)} %param.14) | data formatting | bytes 393216 | tf_op args[6]
  3.0 2.5 %file_lists.1 = (s32[16,8,256]{2,1,0:T(8,128)}, s32[16,8,128]{2,1,0:T(8,128)}) custom-call(s32[1]{0:T(128)S(6)} %copy.15.tile_count, s32[64]{0:T(128)} %hour_tiles.1, s32[64]{0:T(128)} %port_tiles.1, s32[64,3,256]{2,1,0:T(4,128)} %copy.12.coords, s32[64,256]{1,0:T(8,128)} %counts.1), custom_call_target="tpu_custom_call" | custom-call | tf_op jit(solution)/shard_map/file_lists/pallas_call | solution.py:70
  5.5 39.2 %gather_rows.1 = (bf16[16,640,256]{2,1,0:T(8,128)(2,1)}, s32[16,8,256]{2,1,0:T(8,128)}, s32[16,8,128]{2,1,0:T(8,128)}) custom-call(bf16[512,256]{1,0:T(8,128)(2,1)} %hour.1, bf16[128,256]{1,0:T(8,128)(2,1)} %block.1, s32[16,8,256]{2,1,0:T(8,128)} %get-tuple-element.12.box, s32[16,8,128]{2,1,0:T(8,128)} %get-tuple-element.13.code), custom_call_target="tpu_custom_call" | custom-call | tf_op jit(solution)/shard_map/gather_rows/pallas_call | solution.py:208
  44.7 1.2 slice_reduce_fusion
  45.9 0.1 reshape_squeeze.3.codes
  46.0 0.0 copy-start
  46.0 2.5 %copy-done = bf16[16,640,256]{2,1,0:T(8,128)(2,1)S(1)} copy-done((bf16[16,640,256]{2,1,0:T(8,128)(2,1)S(1)}, bf16[16,640,256]{2,1,0:T(8,128)(2,1)}, u32[]{:S(2)}) %copy-start) | copy-done | bytes 5242904
  48.5 0.0 copy-start.1
  48.5 1.6 %copy-done.1 = bf16[4096,256]{1,0:T(8,128)(2,1)S(1)} copy-done((bf16[4096,256]{1,0:T(8,128)(2,1)S(1)}, bf16[4096,256]{1,0:T(8,128)(2,1)}, u32[]{:S(2)}) %copy-start.1) | copy-done | bytes 2097176
  50.1 0.0 copy-start.2
  50.1 0.9 copy-done.2
  51.0 33.3 %tile_terms.1 = (f32[16,640,256]{2,1,0:T(8,128)S(1)}, f32[4096,256]{1,0:T(8,128)}) custom-call(s32[64]{0:T(128)S(1)} %reshape_squeeze.3.codes, bf16[16,640,256]{2,1,0:T(8,128)(2,1)S(1)} %copy-done, s32[16,8,256]{2,1,0:T(8,128)S(1)} %copy-done.2, bf16[4096,256]{1,0:T(8,128)(2,1)S(1)} %copy-done.1), custom_call_target="tpu_custom_call" | custom-call | tf_op jit(solution)/shard_map/tile_terms/pallas_call | solution.py:425
  84.3 54.8 %scatter_sums.1 = (f32[512,256]{1,0:T(8,128)S(1)}, f32[128,256]{1,0:T(8,128)S(1)}) custom-call(f32[16,640,256]{2,1,0:T(8,128)S(1)} %get-tuple-element.17.part), custom_call_target="tpu_custom_call" | custom-call | tf_op jit(solution)/shard_map/scatter_sums/pallas_call | solution.py:321
  139.1 0.7 copy.16
  139.8 0.8 copy.17
Async XLA Ops:
  46.0 2.5 %copy-start = (bf16[16,640,256]{2,1,0:T(8,128)(2,1)S(1)}, bf16[16,640,256]{2,1,0:T(8,128)(2,1)}, u32[]{:S(2)}) copy-start(bf16[16,640,256]{2,1,0:T(8,128)(2,1)} %get-tuple-element.15.rows_ref) | copy-start | bytes 15728644
  48.5 1.6 %copy-start.1 = (bf16[4096,256]{1,0:T(8,128)(2,1)S(1)}, bf16[4096,256]{1,0:T(8,128)(2,1)}, u32[]{:S(2)}) copy-start(bf16[4096,256]{1,0:T(8,128)(2,1)} %port_ref.1) | copy-start | bytes 6291460
  50.1 0.9 copy-start.2

commit v4 on v3

--- a/solution.py
+++ b/solution.py
@@ -208,12 +208,12 @@
     return pl.pallas_call(
         functools.partial(gather_kernel, devices),
         out_shape=[
-            jax.ShapeDtypeStruct((devices, rows, hour.shape[1]), hour.dtype),
-            jax.ShapeDtypeStruct(box.shape, box.dtype),
+            pltpu.VMEM((devices, rows, hour.shape[1]), hour.dtype),
+            pltpu.VMEM(box.shape, box.dtype),
             jax.ShapeDtypeStruct(code.shape, code.dtype),
         ],
         in_specs=[pl.BlockSpec(memory_space=pl.ANY)] * 4,
-        out_specs=[pl.BlockSpec(memory_space=pl.ANY)] * 3,
+        out_specs=[pl.BlockSpec(memory_space=pltpu.VMEM)] * 2 + [pl.BlockSpec(memory_space=pl.ANY)],
         scratch_shapes=[
             pltpu.SemaphoreType.DMA((count + 2,)),
             pltpu.SemaphoreType.DMA(sems),
@@ -225,7 +225,9 @@
             pltpu.SemaphoreType.DMA((2, devices - 1)),
             pltpu.SemaphoreType.DMA((2, devices - 1)),
         ],
-        compiler_params=pltpu.CompilerParams(collective_id=0, has_side_effects=True),
+        compiler_params=pltpu.CompilerParams(
+            collective_id=0, has_side_effects=True, vmem_limit_bytes=8 * 2**20
+        ),
         name="gather_rows",
     )(hour, block, box, code)
 

time: 142 us -> 147 us (1.035)
  local copies, waits for them, and re-layouts: 9.47 us -> 13.5 us
    unnamed x9 -> x17, local copies, waits for them, and re-layouts: 8.19 us -> 13.1 us
    pallas_call x1, Pallas kernels: 54.8 us -> 56.5 us  [scatter(): pl.pallas_call(functools.partial(scatter_kernel, devices, scale), out_sha...]
where the time goes in v4:
time: 147 us; the launch traced here: 145 us
  Pallas kernels  130 us (88%)
  local copies, waits for them, and re-layouts  13.5 us (9%)
    pallas_call x1, Pallas kernels, scatter(): pl.pallas_call(functools.partial(scatter_kernel, devices, scale), out_sha...  56.5 us
    pallas_call x1, Pallas kernels, gather(): pl.pallas_call(functools.partial(gather_kernel, devices), out_shape=[pltp...  38.2 us
    pallas_call x1, Pallas kernels, tiles(): pl.pallas_call(functools.partial(tile_kernel, per_peer, hours, scale), ou...  33.3 us
    unnamed x17, local copies, waits for them, and re-layouts  13.1 us

profile of v4, /device:TPU:0, one launch (start us, length us, event | category | flops | bytes accessed | tf_op | source)
XLA Modules:
  0.0 145.4 jit_solution(7964499257911235808)
XLA Ops:
  1.3 1.8 %copy.12.coords = s32[64,3,256]{2,1,0:T(4,128)} copy(s32[64,3,256]{2,0,1:T(8,128)} %param.14) | data formatting | bytes 393216 | tf_op args[6]
  3.0 2.5 %file_lists.1 = (s32[16,8,256]{2,1,0:T(8,128)}, s32[16,8,128]{2,1,0:T(8,128)}) custom-call(s32[1]{0:T(128)S(6)} %copy.15.tile_count, s32[64]{0:T(128)} %hour_tiles.1, s32[64]{0:T(128)} %port_tiles.1, s32[64,3,256]{2,1,0:T(4,128)} %copy.12.coords, s32[64,256]{1,0:T(8,128)} %counts.1), custom_call_target="tpu_custom_call" | custom-call | tf_op jit(solution)/shard_map/file_lists/pallas_call | solution.py:70
  5.5 0.0 copy-start.3
  5.5 0.9 copy-done.3
  6.5 0.0 copy-start.4
  6.5 0.9 copy-done.4
  7.4 0.0 copy-start.5
  7.4 0.8 copy-done.5
  8.2 0.0 copy-start.6
  8.2 0.8 copy-done.6
  9.0 38.2 %gather_rows.1 = (bf16[16,640,256]{2,1,0:T(8,128)(2,1)S(1)}, s32[16,8,256]{2,1,0:T(8,128)S(1)}, s32[16,8,128]{2,1,0:T(8,128)S(1)}) custom-call(bf16[512,256]{1,0:T(8,128)(2,1)S(1)} %copy-done.3, bf16[128,256]{1,0:T(8,128)(2,1)S(1)} %copy-done.5, s32[16,8,256]{2,1,0:T(8,128)S(1)} %copy-done.4, s32[16,8,128]{2,1,0:T(8,128)S(1)} %copy-done.6), custom_call_target="tpu_custom_call" | custom-call | tf_op jit(solution)/shard_map/gather_rows/pallas_call | solution.py:208
  47.3 0.0 copy-start
  47.3 2.3 %copy-done = bf16[16,640,256]{2,1,0:T(8,128)(2,1)} copy-done((bf16[16,640,256]{2,1,0:T(8,128)(2,1)}, bf16[16,640,256]{2,1,0:T(8,128)(2,1)S(1)}, u32[]{:S(2)}) %copy-start) | copy-done | bytes 5242904
  49.6 0.3 slice_reduce_fusion
  49.9 0.1 reshape_squeeze.3.codes
  50.0 0.0 copy-start.1
  50.0 2.5 %copy-done.1 = bf16[16,640,256]{2,1,0:T(8,128)(2,1)S(1)} copy-done((bf16[16,640,256]{2,1,0:T(8,128)(2,1)S(1)}, bf16[16,640,256]{2,1,0:T(8,128)(2,1)}, u32[]{:S(2)}) %copy-start.1) | copy-done | bytes 5242904
  52.5 0.0 copy-start.2
  52.5 1.6 %copy-done.2 = bf16[4096,256]{1,0:T(8,128)(2,1)S(1)} copy-done((bf16[4096,256]{1,0:T(8,128)(2,1)S(1)}, bf16[4096,256]{1,0:T(8,128)(2,1)}, u32[]{:S(2)}) %copy-start.2) | copy-done | bytes 2097176
  54.1 33.3 %tile_terms.1 = (f32[16,640,256]{2,1,0:T(8,128)S(1)}, f32[4096,256]{1,0:T(8,128)}) custom-call(s32[64]{0:T(128)S(1)} %reshape_squeeze.3.codes, bf16[16,640,256]{2,1,0:T(8,128)(2,1)S(1)} %copy-done.1, s32[16,8,256]{2,1,0:T(8,128)S(1)} %get-tuple-element.16.box_ref, bf16[4096,256]{1,0:T(8,128)(2,1)S(1)} %copy-done.2), custom_call_target="tpu_custom_call" | custom-call | tf_op jit(solution)/shard_map/tile_terms/pallas_call | solution.py:427
  87.4 56.5 %scatter_sums.1 = (f32[512,256]{1,0:T(8,128)S(1)}, f32[128,256]{1,0:T(8,128)S(1)}) custom-call(f32[16,640,256]{2,1,0:T(8,128)S(1)} %get-tuple-element.17.part), custom_call_target="tpu_custom_call" | custom-call | tf_op jit(solution)/shard_map/scatter_sums/pallas_call | solution.py:323
  143.9 0.7 copy.16
  144.6 0.8 copy.17
Async XLA Ops:
  5.5 0.9 copy-start.3
  6.5 0.9 copy-start.4
  7.4 0.8 copy-start.5
  8.2 0.8 copy-start.6
  47.3 2.3 %copy-start = (bf16[16,640,256]{2,1,0:T(8,128)(2,1)}, bf16[16,640,256]{2,1,0:T(8,128)(2,1)S(1)}, u32[]{:S(2)}) copy-start(bf16[16,640,256]{2,1,0:T(8,128)(2,1)S(1)} %get-tuple-element.15.rows_ref) | copy-start | bytes 15728644
  50.0 2.5 %copy-start.1 = (bf16[16,640,256]{2,1,0:T(8,128)(2,1)S(1)}, bf16[16,640,256]{2,1,0:T(8,128)(2,1)}, u32[]{:S(2)}) copy-start(bf16[16,640,256]{2,1,0:T(8,128)(2,1)} %copy-done) | copy-start | bytes 15728644
  52.5 1.6 %copy-start.2 = (bf16[4096,256]{1,0:T(8,128)(2,1)S(1)}, bf16[4096,256]{1,0:T(8,128)(2,1)}, u32[]{:S(2)}) copy-start(bf16[4096,256]{1,0:T(8,128)(2,1)} %port_ref.1) | copy-start | bytes 6291460
